TPU v7x, 512 devices: a whole 4x4x16 slice. The times are simulated.
512 devices in a mesh: depth: 64 (over x_hi, z, core), lat: 8 (over y, x_lo).
Axes of the slice: x: 4 (x_hi: 2, x_lo: 2; x = x_hi * 2 + x_lo), y: 4, z: 16, core: 2. Of those that a mesh axis runs over, the one named last changes fastest.
Arguments:
- in_flight: float32 [64, 4, 256, 256], P('depth', None, 'lat'), may hold values from -6 to 6
- entering: float32 [2, 4, 256, 256], P(None, None, 'lat'), may hold values from -6 to 6
- classes: int32 [64, 256, 256], P('depth', 'lat'), may hold values from 0 to 31
- freq_phase: float32 [66], replicated, may hold values from 4 to 8.5
- class_slowness: float32 [32], replicated, may hold values from 0.8 to 1.4
Outputs:
- images: float32 [64, 8, 256, 256], P('depth', None, 'lat')
- wave_out: float32 [64, 4, 256, 256], P('depth', None, 'lat')
All inputs are finite; a program needn't handle non-finite values.
Results may differ from a plain program's by a relative error of at most 0.0003.
Values sent between devices are 32-bit elements; how exact they have to be, the bound alone decides.
A program may use at most 64 MiB of HBM per device.

v0:
```python
import jax
import jax.numpy as jnp
from jax import lax
from jax.experimental import pallas as pl
from jax.experimental.pallas import tpu as pltpu
from jax.sharding import PartitionSpec as P

TERMS = 16
OFFSETS = 8
TURNS = 3
STRIP = 32
HALO = 19
ROWS = STRIP + 2 * HALO
FOLD = ROWS // 2
REACH = 15
KEPT = FOLD - REACH
PLANE = 48
MESH = pl.DeviceIdType.MESH

hale_weight = 0.0255
centre_weight = -0.5 + hale_weight
edge_weight = 0.25 - 0.5 * hale_weight
corner_weight = 0.125 + 0.25 * hale_weight
kappa = edge_weight / corner_weight
delta = centre_weight - edge_weight * kappa
miller_start = 32


def lane_gather(x, idx):
    numbers = lax.GatherDimensionNumbers(
        offset_dims=(),
        collapsed_slice_dims=(1,),
        start_index_map=(1,),
        operand_batching_dims=(0,),
        start_indices_batching_dims=(0,),
    )
    return lax.gather(
        x, idx[:, :, None], numbers, (1, 1), mode=lax.GatherScatterMode.PROMISE_IN_BOUNDS
    )


def kernel(
    inflight_ref, entering_ref, classes_ref, freq_ref, slow_ref,
    images_ref, wave_ref,
    raw, raw_cls, cls_up, cls_dn, pr, adv, ta, tb, acc_e, acc_o, coef, cls, table, std, img, wout,
    in_sem, out_sem, ssem, rsem, esem, cssem, crsem,
):
    d = lax.axis_index("depth")
    l = lax.axis_index("lat")
    D = lax.axis_size("depth")
    L = lax.axis_size("lat")

    sub = lax.broadcasted_iota(jnp.int32, (8, 128), 0)
    lane = lax.broadcasted_iota(jnp.int32, (8, 128), 1)
    low = sub < 4

    def roll4(x):
        return pltpu.roll(x, 4, 0)

    def load_fields(src, slot):
        return [
            pltpu.make_async_copy(
                src.at[f, :, pl.ds(h * 128, 128)],
                raw.at[slot, pl.ds((h * 4 + f) * STRIP, STRIP)],
                in_sem.at[slot, h * 4 + f],
            )
            for h in range(2)
            for f in range(4)
        ]

    for c in load_fields(inflight_ref.at[0], 0):
        c.start()
    cls_copy = pltpu.make_async_copy(classes_ref.at[0], raw_cls, in_sem.at[TURNS, 0])
    cls_copy.start()

    @pl.when(d == 0)
    def _():
        for t in range(TURNS - 1):
            for c in load_fields(entering_ref.at[t], t + 1):
                c.start()

    bar = pltpu.get_barrier_semaphore()
    has_up, has_dn, has_next, has_prev = l > 0, l < L - 1, d < D - 1, d > 0

    def greet(cond, dd, dl):
        @pl.when(cond)
        def _():
            pl.semaphore_signal(bar, inc=1, device_id=(d + dd, l + dl), device_id_type=MESH)

    greet(has_up, 0, -1)
    greet(has_dn, 0, 1)
    greet(has_prev, -1, 0)
    greet(jnp.logical_and(has_prev, has_up), -1, -1)
    greet(jnp.logical_and(has_prev, has_dn), -1, 1)

    zero = jnp.zeros((8, 128), jnp.float32)

    @pl.when(l == 0)
    def _():
        for t in range(TURNS):
            for i in range(HALO):
                pr[t, i] = zero
        cls_up[...] = jnp.zeros_like(cls_up)

    @pl.when(l == L - 1)
    def _():
        for t in range(TURNS):
            for i in range(HALO):
                pr[t, HALO + STRIP + i] = zero
        cls_dn[...] = jnp.zeros_like(cls_dn)

    keep = jnp.where(
        low, jnp.where(l > 0, 1.0, 0.0).astype(jnp.float32), jnp.where(l < L - 1, 1.0, 0.0).astype(jnp.float32)
    )

    pack_idx = 2 * jnp.bitwise_and(lane, 63) + jnp.where(low, 0, 1)
    pack_direct = (lane < 64) == low

    def pack_fields(slot):
        def body(y, _):
            v = raw[slot, pl.ds(y, 8, stride=STRIP), :]
            a = lane_gather(v, pack_idx)
            b = lane_gather(roll4(v), pack_idx)
            pr[slot, HALO + y] = jnp.where(pack_direct, a, b)
            return 0

        lax.fori_loop(0, STRIP, body, 0, unroll=8)

    for c in load_fields(inflight_ref.at[0], 0):
        c.wait()
    pack_fields(0)

    n_lat = has_up.astype(jnp.int32) + has_dn.astype(jnp.int32)
    pl.semaphore_wait(bar, n_lat + has_next.astype(jnp.int32) * (1 + n_lat))
    cls_copy.wait()

    def to_up(src, slot, dd, sem):
        return pltpu.make_async_remote_copy(
            src, pr.at[slot, pl.ds(HALO + STRIP, HALO)], sem, rsem.at[slot, 1],
            device_id=(d + dd, l - 1), device_id_type=MESH,
        )

    def to_dn(src, slot, dd, sem):
        return pltpu.make_async_remote_copy(
            src, pr.at[slot, pl.ds(0, HALO)], sem, rsem.at[slot, 2],
            device_id=(d + dd, l + 1), device_id_type=MESH,
        )

    def lat_sends(slot):
        up = to_up(pr.at[slot, pl.ds(HALO, HALO)], slot, 0, esem.at[slot, 0])
        dn = to_dn(pr.at[slot, pl.ds(STRIP, HALO)], slot, 0, esem.at[slot, 1])
        return up, dn

    def cls_sends():
        up = pltpu.make_async_remote_copy(
            raw_cls.at[pl.ds(0, 8)], cls_dn, cssem.at[0], crsem.at[0], device_id=(d, l - 1), device_id_type=MESH
        )
        dn = pltpu.make_async_remote_copy(
            raw_cls.at[pl.ds(STRIP - 8, 8)], cls_up, cssem.at[1], crsem.at[1], device_id=(d, l + 1), device_id_type=MESH
        )
        return up, dn

    @pl.when(has_up)
    def _():
        lat_sends(0)[0].start()
        cls_sends()[0].start()

    @pl.when(has_dn)
    def _():
        lat_sends(0)[1].start()
        cls_sends()[1].start()

    @pl.when(d == 0)
    def _():
        for t in range(1, TURNS):
            for c in load_fields(entering_ref.at[t - 1], t):
                c.wait()
            pack_fields(t)

    @pl.when(jnp.logical_and(d == 0, has_up))
    def _():
        for t in range(1, TURNS):
            lat_sends(t)[0].start()

    @pl.when(jnp.logical_and(d == 0, has_dn))
    def _():
        for t in range(1, TURNS):
            lat_sends(t)[1].start()

    cid = jnp.bitwise_and(lane, 31)
    slow = jnp.zeros((8, 128), jnp.float32)
    for c in range(32):
        slow = jnp.where(cid == c, slow_ref[c], slow)
    for t in range(TURNS):
        inv = 1.0 / (freq_ref[t + D - 1 - d] * slow)
        values = [None] * (miller_start + 1)
        upper = jnp.zeros_like(inv)
        current = jnp.ones_like(inv)
        values[miller_start] = current
        for k in range(miller_start, 0, -1):
            lower = (2.0 * k * inv) * current - upper
            values[k - 1] = lower
            upper, current = current, lower
        evens = values[2]
        for k in range(4, miller_start + 1, 2):
            evens = evens + values[k]
        scale = 1.0 / (values[0] + 2.0 * evens)
        for k in range(TERMS):
            sign = -1.0 if (k // 2) % 2 else 1.0
            table[t, k] = values[k] * scale * (sign if k == 0 else 2.0 * sign)

    half_lane = lane < 64
    even_idx = 2 * jnp.bitwise_and(lane, 63)

    def fold_classes(i, top, top_row, bottom, bottom_row):
        sides = []
        for h in range(2):
            a = jnp.broadcast_to(top[pl.ds(top_row, 1), h * 128 : (h + 1) * 128], (8, 128))
            b = jnp.broadcast_to(bottom[pl.ds(bottom_row, 1), h * 128 : (h + 1) * 128], (8, 128))
            sides.append(jnp.where(low, a, b))
        for p in range(2):
            cls[i, p] = jnp.where(
                half_lane, lane_gather(sides[0], even_idx + p), lane_gather(sides[1], even_idx + p)
            )

    @pl.when(has_up)
    def _():
        cls_sends()[1].wait_recv()

    @pl.when(has_dn)
    def _():
        cls_sends()[0].wait_recv()

    for i in range(4):
        fold_classes(i, cls_up, 4 + i, cls_dn, 3 - i)
    for i in range(4, KEPT):
        fold_classes(i, raw_cls, i - 4, raw_cls, STRIP + 3 - i)

    def look_up(t):
        def body(i, _):
            for p in range(2):
                c = cls[i, p]
                for k in range(TERMS):
                    coef[k, i, p] = lane_gather(table[t, k], c)
            return 0

        lax.fori_loop(0, KEPT, body, 0)

    def step(cur, prev, low_row, k, first, even):
        acc = acc_e if even else acc_o
        c1 = corner_weight * (1.0 if first else 2.0)
        c2 = delta * (1.0 if first else 2.0)
        above = [cur[low_row - 1, p] for p in range(2)]
        here = [cur[low_row, p] for p in range(2)]
        for i in range(low_row, FOLD):
            if i < FOLD - 1:
                below = [cur[i + 1, p] for p in range(2)]
            else:
                below = [roll4(v) for v in here]
            w = [(above[p] + below[p]) + kappa * here[p] for p in range(2)]
            from_odd = jnp.where(lane == 0, 0.0, pltpu.roll(w[1], 1, 1))
            from_even = jnp.where(lane == 127, 0.0, pltpu.roll(w[0], 127, 1))
            x = [from_odd + w[1], w[0] + from_even]
            for p in range(2):
                f = c1 * (x[p] + kappa * w[p]) + c2 * here[p]
                if not first:
                    f = f - prev[i, p]
                if i < HALO:
                    f = f * keep
                prev[i, p] = f
                if i >= REACH:
                    j = i - REACH
                    if first:
                        acc[j, p] = coef[k, j, p] * f
                    else:
                        acc[j, p] = acc[j, p] + coef[k, j, p] * f
            above, here = here, below

    swap_sign = jnp.where(jnp.logical_or(jnp.bitwise_and(sub, 3) == 0, jnp.bitwise_and(sub, 3) == 3), -1.0, 1.0).astype(jnp.float32)
    even_sub = jnp.bitwise_and(sub, 1) == 0

    def extrapolate(t):
        def unfold(i):
            a = pr[t, i]
            b = pr[t, ROWS - 1 - i]
            return jnp.where(low, a, roll4(b)), jnp.where(low, roll4(a), b)

        def body0(i, _):
            e, o = unfold(i)
            ta[i, 0] = e
            ta[i, 1] = o
            return 0

        def body1(i, _):
            e, o = unfold(i)
            ta[i, 0] = e
            ta[i, 1] = o
            acc_e[i - REACH, 0] = coef[0, i - REACH, 0] * e
            acc_e[i - REACH, 1] = coef[0, i - REACH, 1] * o
            return 0

        lax.fori_loop(0, REACH, body0, 0, unroll=5)
        lax.fori_loop(REACH, FOLD, body1, 0, unroll=5)

        step(ta, tb, 1, 1, True, False)

        def pair(base):
            def body(n, _):
                k = base + 2 * n
                step(tb, ta, base, k, False, True)
                step(ta, tb, base + 1, k + 1, False, False)
                return 0

            return body

        lax.fori_loop(0, 2, pair(2), 0)
        lax.fori_loop(0, 2, pair(6), 0)
        lax.fori_loop(0, 2, pair(10), 0)
        lax.fori_loop(0, 1, pair(14), 0)

        def join(i, _):
            out = []
            for p in range(2):
                o = acc_o[i, p]
                swapped = jnp.where(even_sub, pltpu.roll(o, 7, 0), pltpu.roll(o, 1, 0))
                out.append(acc_e[i, p] + swap_sign * swapped)
            adv[t, i] = jnp.where(low, out[0], roll4(out[1]))
            adv[t, 2 * KEPT - 1 - i] = jnp.where(low, roll4(out[0]), out[1])
            return 0

        lax.fori_loop(0, KEPT, join, 0, unroll=5)

    def correlate(t):
        def spread(r, _):
            std[pl.ds(r, 8, stride=PLANE), :] = adv[t, r]
            return 0

        lax.fori_loop(0, 2 * KEPT, spread, 0, unroll=8)
        for p in range(2):
            for b in range(STRIP // 8):
                for o in range(OFFSETS):
                    g = o - OFFSETS // 2
                    s0 = std[pl.ds((p * 4 + 0) * PLANE + 4 - g + 8 * b, 8), :]
                    s1 = std[pl.ds((p * 4 + 1) * PLANE + 4 - g + 8 * b, 8), :]
                    r0 = std[pl.ds((p * 4 + 2) * PLANE + 4 + g + 8 * b, 8), :]
                    r1 = std[pl.ds((p * 4 + 3) * PLANE + 4 + g + 8 * b, 8), :]
                    value = s0 * r0 + s1 * r1
                    if t > 0:
                        value = value + img[p, o, b]
                    img[p, o, b] = value

    def hand_over(t):
        n = t + 1
        strip = pltpu.make_async_remote_copy(
            adv.at[t, pl.ds(4, STRIP)], pr.at[n, pl.ds(HALO, STRIP)], ssem.at[t, 0], rsem.at[n, 0],
            device_id=(d + 1, l), device_id_type=MESH,
        )
        up = to_up(adv.at[t, pl.ds(4, HALO)], n, 1, ssem.at[t, 1])
        dn = to_dn(adv.at[t, pl.ds(4 + STRIP - HALO, HALO)], n, 1, ssem.at[t, 2])
        return strip, up, dn

    next_up = jnp.logical_and(has_next, has_up)
    next_dn = jnp.logical_and(has_next, has_dn)

    def for_each_send(t, act):
        for cond, which in ((next_up, 1), (next_dn, 2), (has_next, 0)):
            @pl.when(cond)
            def _():
                act(hand_over(t)[which])

    def wait_halo(t):
        @pl.when(has_dn)
        def _():
            lat_sends(t)[0].wait_recv()

        @pl.when(has_up)
        def _():
            lat_sends(t)[1].wait_recv()

    look_up(0)
    for t in range(TURNS):
        wait_halo(t)
        if t > 0:
            @pl.when(has_prev)
            def _():
                hand_over(t - 1)[0].wait_recv()
        extrapolate(t)
        if t + 1 < TURNS:
            for_each_send(t, lambda c: c.start())
            correlate(t)
            look_up(t + 1)

    join_idx = lax.shift_right_logical(lane, 1) + jnp.where(low, 0, 64)
    join_direct = (jnp.bitwise_and(lane, 1) == 0) == low

    def put(y, _):
        v = adv[TURNS - 1, 4 + y]
        a = lane_gather(v, join_idx)
        b = lane_gather(roll4(v), join_idx)
        wout[pl.ds(y, 8, stride=STRIP), :] = jnp.where(join_direct, a, b)
        return 0

    lax.fori_loop(0, STRIP, put, 0, unroll=8)

    def stores():
        return [
            pltpu.make_async_copy(
                wout.at[pl.ds((h * 4 + f) * STRIP, STRIP)],
                wave_ref.at[0, f, :, pl.ds(h * 128, 128)],
                out_sem.at[h * 4 + f],
            )
            for h in range(2)
            for f in range(4)
        ]

    for c in stores():
        c.start()
    correlate(TURNS - 1)
    half_idx = lax.shift_right_logical(lane, 1)
    even_lane = jnp.bitwise_and(lane, 1) == 0
    for o in range(OFFSETS):
        for b in range(STRIP // 8):
            e, q = img[0, o, b], img[1, o, b]
            for h in range(2):
                images_ref[0, o, pl.ds(8 * b, 8), pl.ds(128 * h, 128)] = jnp.where(
                    even_lane, lane_gather(e, half_idx + 64 * h), lane_gather(q, half_idx + 64 * h)
                )

    @pl.when(has_up)
    def _():
        lat_sends(0)[0].wait_send()
        cls_sends()[0].wait_send()

    @pl.when(has_dn)
    def _():
        lat_sends(0)[1].wait_send()
        cls_sends()[1].wait_send()

    @pl.when(jnp.logical_and(d == 0, has_up))
    def _():
        for t in range(1, TURNS):
            lat_sends(t)[0].wait_send()

    @pl.when(jnp.logical_and(d == 0, has_dn))
    def _():
        for t in range(1, TURNS):
            lat_sends(t)[1].wait_send()

    for t in range(TURNS - 1):
        for_each_send(t, lambda c: c.wait_send())
    for c in stores():
        c.wait()


def local(in_flight, entering, classes, freq_phase, class_slowness):
    any_space = pl.BlockSpec(memory_space=pl.ANY)
    smem = pl.BlockSpec(memory_space=pltpu.SMEM)
    f32, i32 = jnp.float32, jnp.int32
    dma = pltpu.SemaphoreType.DMA
    return pl.pallas_call(
        kernel,
        out_shape=(
            jax.ShapeDtypeStruct((1, OFFSETS, STRIP, 256), f32),
            jax.ShapeDtypeStruct((1, 4, STRIP, 256), f32),
        ),
        in_specs=[any_space, any_space, any_space, smem, smem],
        out_specs=(pl.BlockSpec(memory_space=pltpu.VMEM), any_space),
        scratch_shapes=[
            pltpu.VMEM((TURNS, 8 * STRIP, 128), f32),
            pltpu.VMEM((STRIP, 256), i32),
            pltpu.VMEM((8, 256), i32),
            pltpu.VMEM((8, 256), i32),
            pltpu.VMEM((TURNS, ROWS, 8, 128), f32),
            pltpu.VMEM((TURNS, 2 * KEPT, 8, 128), f32),
            pltpu.VMEM((FOLD, 2, 8, 128), f32),
            pltpu.VMEM((FOLD, 2, 8, 128), f32),
            pltpu.VMEM((KEPT, 2, 8, 128), f32),
            pltpu.VMEM((KEPT, 2, 8, 128), f32),
            pltpu.VMEM((TERMS, KEPT, 2, 8, 128), f32),
            pltpu.VMEM((KEPT, 2, 8, 128), i32),
            pltpu.VMEM((TURNS, TERMS, 8, 128), f32),
            pltpu.VMEM((8 * PLANE, 128), f32),
            pltpu.VMEM((2, OFFSETS, STRIP // 8, 8, 128), f32),
            pltpu.VMEM((8 * STRIP, 128), f32),
            dma((TURNS + 1, 8)),
            dma((8,)),
            dma((TURNS - 1, 3)),
            dma((TURNS, 3)),
            dma((TURNS, 2)),
            dma((2,)),
            dma((2,)),
        ],
        compiler_params=pltpu.CompilerParams(
            collective_id=0, has_side_effects=True, vmem_limit_bytes=40 * 2**20
        ),
        cost_estimate=pl.CostEstimate(flops=60_000_000, bytes_accessed=1_000_000, transcendentals=0),
    )(in_flight, entering, classes, freq_phase, class_slowness)


def solution(mesh):
    in_specs = (
        P("depth", None, "lat", None),
        P(None, None, "lat", None),
        P("depth", "lat", None),
        P(),
        P(),
    )
    out_specs = (P("depth", None, "lat", None), P("depth", None, "lat", None))
    return jax.shard_map(local, mesh=mesh, in_specs=in_specs, out_specs=out_specs, check_vma=False)
```

profile of v0, /device:TPU:22, one launch (start us, length us, event | category | flops | bytes accessed | tf_op | source)
XLA Modules:
  0.0 44.2 jit_solution(7664245989581587704)
XLA Ops:
  0.6 0.0 copy-start
  0.6 0.9 %copy-done = f32[2,4,32,256]{3,2,1,0:T(8,128)S(1)} copy-done((f32[2,4,32,256]{3,2,1,0:T(8,128)S(1)}, f32[2,4,32,256]{3,2,1,0:T(8,128)}, u32[]{:S(2)}) %copy-start) | copy-done | bytes 262168
  1.6 0.0 copy-start.1
  1.6 0.9 %copy-done.1 = f32[1,4,32,256]{3,2,1,0:T(8,128)S(1)} copy-done((f32[1,4,32,256]{3,2,1,0:T(8,128)S(1)}, f32[1,4,32,256]{3,2,1,0:T(8,128)}, u32[]{:S(2)}) %copy-start.1) | copy-done | bytes 131096
  2.5 0.0 copy-start.2
  2.5 0.8 %copy-done.2 = s32[1,32,256]{2,1,0:T(8,128)S(1)} copy-done((s32[1,32,256]{2,1,0:T(8,128)S(1)}, s32[1,32,256]{2,1,0:T(8,128)}, u32[]{:S(2)}) %copy-start.2) | copy-done | bytes 32792
  3.2 0.0 copy-start.3
  3.2 0.7 %copy-done.3 = f32[66]{0:T(128)S(1)} copy-done((f32[66]{0:T(128)S(1)}, f32[66]{0:T(128)}, u32[]{:S(2)}) %copy-start.3) | copy-done | bytes 288
  3.9 0.0 copy-start.4
  3.9 0.7 %copy-done.4 = f32[32]{0:T(128)S(1)} copy-done((f32[32]{0:T(128)S(1)}, f32[32]{0:T(128)}, u32[]{:S(2)}) %copy-start.4) | copy-done | bytes 152
  4.6 38.2 %shard_map.68 = (f32[1,8,32,256]{3,2,1,0:T(8,128)S(1)}, f32[1,4,32,256]{3,2,1,0:T(8,128)S(1)}) custom-call(f32[1,4,32,256]{3,2,1,0:T(8,128)S(1)} %copy-done.1, f32[2,4,32,256]{3,2,1,0:T(8,128)S(1)} %copy-done, s32[1,32,256]{2,1,0:T(8,128)S(1)} %copy-done.2, f32[66]{0:T(128)S(1)} %copy-done.3, f32[32]{0:T(128)S(1)} %copy-done.4), custom_call_target="tpu_custom_call" | custom-call | flops 60000000 | bytes 1000000 | tf_op jit(solution)/shard_map/pallas_call | solution.py:460
  42.8 0.7 %copy.9 = f32[1,8,32,256]{3,2,1,0:T(8,128)} copy(f32[1,8,32,256]{3,2,1,0:T(8,128)S(1)} %get-tuple-element.4) | data formatting | bytes 524288
  43.5 0.7 %copy.10 = f32[1,4,32,256]{3,2,1,0:T(8,128)} copy(f32[1,4,32,256]{3,2,1,0:T(8,128)S(1)} %get-tuple-element.5) | data formatting | bytes 262144
Async XLA Ops:
  0.6 1.0 %copy-start = (f32[2,4,32,256]{3,2,1,0:T(8,128)S(1)}, f32[2,4,32,256]{3,2,1,0:T(8,128)}, u32[]{:S(2)}) copy-start(f32[2,4,32,256]{3,2,1,0:T(8,128)} %entering_ref.1) | copy-start | bytes 786436
  1.6 0.9 %copy-start.1 = (f32[1,4,32,256]{3,2,1,0:T(8,128)S(1)}, f32[1,4,32,256]{3,2,1,0:T(8,128)}, u32[]{:S(2)}) copy-start(f32[1,4,32,256]{3,2,1,0:T(8,128)} %inflight_ref.1) | copy-start | bytes 393220
  2.5 0.8 %copy-start.2 = (s32[1,32,256]{2,1,0:T(8,128)S(1)}, s32[1,32,256]{2,1,0:T(8,128)}, u32[]{:S(2)}) copy-start(s32[1,32,256]{2,1,0:T(8,128)} %classes_ref.1) | copy-start | bytes 98308
  3.2 0.7 %copy-start.3 = (f32[66]{0:T(128)S(1)}, f32[66]{0:T(128)}, u32[]{:S(2)}) copy-start(f32[66]{0:T(128)} %freq_ref.1) | copy-start | bytes 796
  3.9 0.7 %copy-start.4 = (f32[32]{0:T(128)S(1)}, f32[32]{0:T(128)}, u32[]{:S(2)}) copy-start(f32[32]{0:T(128)} %slow_ref.1) | copy-start | bytes 388
where the time goes:
time: 44.4 us; the launch traced here: 44.2 us
  Pallas kernels  38.2 us (86%)
  local copies, waits for them, and re-layouts  5.27 us (12%)
  between operations  0.65 us (1%)
    pallas_call x1, Pallas kernels, local(): pl.pallas_call(kernel, out_shape=(jax.ShapeDtypeStruct((1, OFFSETS, STRIP...  38.2 us
    unnamed x12, local copies, waits for them, and re-layouts  5.27 us

commit v1 on v0

--- a/solution.py
+++ b/solution.py
@@ -97,17 +97,24 @@
 
     @pl.when(l == 0)
     def _():
-        for t in range(TURNS):
-            for i in range(HALO):
-                pr[t, i] = zero
         cls_up[...] = jnp.zeros_like(cls_up)
 
     @pl.when(l == L - 1)
     def _():
-        for t in range(TURNS):
-            for i in range(HALO):
-                pr[t, HALO + STRIP + i] = zero
         cls_dn[...] = jnp.zeros_like(cls_dn)
+
+    def reflect(t):
+        @pl.when(l == 0)
+        def _():
+            pr[t, HALO - 1] = zero
+            for j in range(1, HALO):
+                pr[t, HALO - 1 - j] = -pr[t, HALO - 1 + j]
+
+        @pl.when(l == L - 1)
+        def _():
+            pr[t, HALO + STRIP] = zero
+            for j in range(1, HALO):
+                pr[t, HALO + STRIP + j] = -pr[t, HALO + STRIP - j]
 
     keep = jnp.where(
         low, jnp.where(l > 0, 1.0, 0.0).astype(jnp.float32), jnp.where(l < L - 1, 1.0, 0.0).astype(jnp.float32)
@@ -246,13 +253,14 @@
 
         lax.fori_loop(0, KEPT, body, 0)
 
-    def step(cur, prev, low_row, k, first, even):
+    def step(cur, prev, low_row, top_row, k):
+        first, even = k == 1, k % 2 == 0
         acc = acc_e if even else acc_o
         c1 = corner_weight * (1.0 if first else 2.0)
         c2 = delta * (1.0 if first else 2.0)
         above = [cur[low_row - 1, p] for p in range(2)]
         here = [cur[low_row, p] for p in range(2)]
-        for i in range(low_row, FOLD):
+        for i in range(low_row, top_row):
             if i < FOLD - 1:
                 below = [cur[i + 1, p] for p in range(2)]
             else:
@@ -265,8 +273,6 @@
                 f = c1 * (x[p] + kappa * w[p]) + c2 * here[p]
                 if not first:
                     f = f - prev[i, p]
-                if i < HALO:
-                    f = f * keep
                 prev[i, p] = f
                 if i >= REACH:
                     j = i - REACH
@@ -279,56 +285,40 @@
     swap_sign = jnp.where(jnp.logical_or(jnp.bitwise_and(sub, 3) == 0, jnp.bitwise_and(sub, 3) == 3), -1.0, 1.0).astype(jnp.float32)
     even_sub = jnp.bitwise_and(sub, 1) == 0
 
-    def extrapolate(t):
+    def extrapolate(t, halo_wait):
         def unfold(i):
             a = pr[t, i]
             b = pr[t, ROWS - 1 - i]
             return jnp.where(low, a, roll4(b)), jnp.where(low, roll4(a), b)
 
-        def body0(i, _):
+        def start(i):
             e, o = unfold(i)
             ta[i, 0] = e
             ta[i, 1] = o
-            return 0
-
-        def body1(i, _):
-            e, o = unfold(i)
-            ta[i, 0] = e
-            ta[i, 1] = o
-            acc_e[i - REACH, 0] = coef[0, i - REACH, 0] * e
-            acc_e[i - REACH, 1] = coef[0, i - REACH, 1] * o
-            return 0
-
-        lax.fori_loop(0, REACH, body0, 0, unroll=5)
-        lax.fori_loop(REACH, FOLD, body1, 0, unroll=5)
-
-        step(ta, tb, 1, 1, True, False)
-
-        def pair(base):
-            def body(n, _):
-                k = base + 2 * n
-                step(tb, ta, base, k, False, True)
-                step(ta, tb, base + 1, k + 1, False, False)
-                return 0
-
-            return body
-
-        lax.fori_loop(0, 2, pair(2), 0)
-        lax.fori_loop(0, 2, pair(6), 0)
-        lax.fori_loop(0, 2, pair(10), 0)
-        lax.fori_loop(0, 1, pair(14), 0)
-
-        def join(i, _):
+            if i >= REACH:
+                acc_e[i - REACH, 0] = coef[0, i - REACH, 0] * e
+                acc_e[i - REACH, 1] = coef[0, i - REACH, 1] * o
+
+        bufs = (ta, tb)
+        halo_wait()
+        reflect(t)
+        for i in range(FOLD):
+            start(i)
+        for k in range(1, TERMS):
+            step(bufs[(k - 1) % 2], bufs[k % 2], k, FOLD, k)
+
+        def join(i, inside):
             out = []
             for p in range(2):
                 o = acc_o[i, p]
                 swapped = jnp.where(even_sub, pltpu.roll(o, 7, 0), pltpu.roll(o, 1, 0))
-                out.append(acc_e[i, p] + swap_sign * swapped)
+                value = acc_e[i, p] + swap_sign * swapped
+                out.append(value if inside else value * keep)
             adv[t, i] = jnp.where(low, out[0], roll4(out[1]))
             adv[t, 2 * KEPT - 1 - i] = jnp.where(low, roll4(out[0]), out[1])
-            return 0
-
-        lax.fori_loop(0, KEPT, join, 0, unroll=5)
+
+        for i in range(KEPT):
+            join(i, i >= HALO - REACH)
 
     def correlate(t):
         def spread(r, _):
@@ -379,12 +369,11 @@
 
     look_up(0)
     for t in range(TURNS):
-        wait_halo(t)
         if t > 0:
             @pl.when(has_prev)
             def _():
                 hand_over(t - 1)[0].wait_recv()
-        extrapolate(t)
+        extrapolate(t, lambda: wait_halo(t))
         if t + 1 < TURNS:
             for_each_send(t, lambda c: c.start())
             correlate(t)
@@ -460,11 +449,11 @@
     return pl.pallas_call(
         kernel,
         out_shape=(
-            jax.ShapeDtypeStruct((1, OFFSETS, STRIP, 256), f32),
-            jax.ShapeDtypeStruct((1, 4, STRIP, 256), f32),
+            pltpu.VMEM((1, OFFSETS, STRIP, 256), f32),
+            pltpu.VMEM((1, 4, STRIP, 256), f32),
         ),
         in_specs=[any_space, any_space, any_space, smem, smem],
-        out_specs=(pl.BlockSpec(memory_space=pltpu.VMEM), any_space),
+        out_specs=(pl.BlockSpec(memory_space=pltpu.VMEM), pl.BlockSpec(memory_space=pltpu.VMEM)),
         scratch_shapes=[
             pltpu.VMEM((TURNS, 8 * STRIP, 128), f32),
             pltpu.VMEM((STRIP, 256), i32),
@@ -491,7 +480,7 @@
             dma((2,)),
         ],
         compiler_params=pltpu.CompilerParams(
-            collective_id=0, has_side_effects=True, vmem_limit_bytes=40 * 2**20
+            collective_id=0, has_side_effects=True, vmem_limit_bytes=56 * 2**20
         ),
         cost_estimate=pl.CostEstimate(flops=60_000_000, bytes_accessed=1_000_000, transcendentals=0),
     )(in_flight, entering, classes, freq_phase, class_slowness)

time: 44.4 us -> 38.5 us (0.87)
  local copies, waits for them, and re-layouts: 5.27 us -> 1.36 us
  Pallas kernels: 38.2 us -> 36.3 us
    unnamed x12 -> x2, local copies, waits for them, and re-layouts: 5.27 us -> 1.36 us
    pallas_call x1, Pallas kernels: 38.2 us -> 36.3 us  [local(): pl.pallas_call(kernel, out_shape=(pltpu.VMEM((1, OFFSETS, STRIP, 256), f3...]
where the time goes in v1:
time: 38.5 us; the launch traced here: 38.3 us
  Pallas kernels  36.3 us (94%)
  local copies, waits for them, and re-layouts  1.36 us (4%)
  between operations  0.64 us (2%)
    pallas_call x1, Pallas kernels, local(): pl.pallas_call(kernel, out_shape=(pltpu.VMEM((1, OFFSETS, STRIP, 256), f3...  36.3 us
    unnamed x2, local copies, waits for them, and re-layouts  1.36 us

profile of v1, /device:TPU:22, one launch (start us, length us, event | category | flops | bytes accessed | tf_op | source)
XLA Modules:
  0.0 38.3 jit_solution(10276444422123469806)
XLA Ops:
  0.6 36.3 %shard_map.68 = (f32[1,8,32,256]{3,2,1,0:T(8,128)S(1)}, f32[1,4,32,256]{3,2,1,0:T(8,128)S(1)}) custom-call(f32[1,4,32,256]{3,2,1,0:T(8,128)} %inflight_ref.1, f32[2,4,32,256]{3,2,1,0:T(8,128)} %entering_ref.1, s32[1,32,256]{2,1,0:T(8,128)} %classes_ref.1, f32[66]{0:T(128)} %freq_ref.1, f32[32]{0:T(128)} %slow_ref.1), custom_call_target="tpu_custom_call" | custom-call | flops 60000000 | bytes 1000000 | tf_op jit(solution)/shard_map/pallas_call | solution.py:449
  37.0 0.7 %copy.9 = f32[1,8,32,256]{3,2,1,0:T(8,128)} copy(f32[1,8,32,256]{3,2,1,0:T(8,128)S(1)} %get-tuple-element.2) | data formatting | bytes 524288
  37.7 0.7 %copy.10 = f32[1,4,32,256]{3,2,1,0:T(8,128)} copy(f32[1,4,32,256]{3,2,1,0:T(8,128)S(1)} %get-tuple-element.3) | data formatting | bytes 262144

commit v2 on v1

--- a/solution.py
+++ b/solution.py
@@ -42,8 +42,8 @@
 def kernel(
     inflight_ref, entering_ref, classes_ref, freq_ref, slow_ref,
     images_ref, wave_ref,
-    raw, raw_cls, cls_up, cls_dn, pr, adv, ta, tb, acc_e, acc_o, coef, cls, table, std, img, wout,
-    in_sem, out_sem, ssem, rsem, esem, cssem, crsem,
+    raw, raw_cls, cls_up, cls_dn, pr, adv, ta, tb, acc_e, acc_o, coef, cls, table, std,
+    in_sem, ssem, rsem, esem, cssem, crsem,
 ):
     d = lax.axis_index("depth")
     l = lax.axis_index("lat")
@@ -320,24 +320,33 @@
         for i in range(KEPT):
             join(i, i >= HALO - REACH)
 
+    join_idx = lax.shift_right_logical(lane, 1) + jnp.where(low, 0, 64)
+    join_direct = (jnp.bitwise_and(lane, 1) == 0) == low
+
     def correlate(t):
         def spread(r, _):
-            std[pl.ds(r, 8, stride=PLANE), :] = adv[t, r]
+            v = adv[t, r]
+            natural = jnp.where(join_direct, lane_gather(v, join_idx), lane_gather(roll4(v), join_idx))
+            std[pl.ds(r, 8, stride=PLANE), :] = natural
             return 0
 
         lax.fori_loop(0, 2 * KEPT, spread, 0, unroll=8)
-        for p in range(2):
+        for h in range(2):
             for b in range(STRIP // 8):
+                rows, columns = pl.ds(8 * b, 8), pl.ds(128 * h, 128)
+                if t == TURNS - 1:
+                    for f in range(4):
+                        wave_ref[0, f, rows, columns] = std[pl.ds((h * 4 + f) * PLANE + 4 + 8 * b, 8), :]
                 for o in range(OFFSETS):
                     g = o - OFFSETS // 2
-                    s0 = std[pl.ds((p * 4 + 0) * PLANE + 4 - g + 8 * b, 8), :]
-                    s1 = std[pl.ds((p * 4 + 1) * PLANE + 4 - g + 8 * b, 8), :]
-                    r0 = std[pl.ds((p * 4 + 2) * PLANE + 4 + g + 8 * b, 8), :]
-                    r1 = std[pl.ds((p * 4 + 3) * PLANE + 4 + g + 8 * b, 8), :]
+                    s0 = std[pl.ds((h * 4 + 0) * PLANE + 4 - g + 8 * b, 8), :]
+                    s1 = std[pl.ds((h * 4 + 1) * PLANE + 4 - g + 8 * b, 8), :]
+                    r0 = std[pl.ds((h * 4 + 2) * PLANE + 4 + g + 8 * b, 8), :]
+                    r1 = std[pl.ds((h * 4 + 3) * PLANE + 4 + g + 8 * b, 8), :]
                     value = s0 * r0 + s1 * r1
                     if t > 0:
-                        value = value + img[p, o, b]
-                    img[p, o, b] = value
+                        value = value + images_ref[0, o, rows, columns]
+                    images_ref[0, o, rows, columns] = value
 
     def hand_over(t):
         n = t + 1
@@ -379,41 +388,7 @@
             correlate(t)
             look_up(t + 1)
 
-    join_idx = lax.shift_right_logical(lane, 1) + jnp.where(low, 0, 64)
-    join_direct = (jnp.bitwise_and(lane, 1) == 0) == low
-
-    def put(y, _):
-        v = adv[TURNS - 1, 4 + y]
-        a = lane_gather(v, join_idx)
-        b = lane_gather(roll4(v), join_idx)
-        wout[pl.ds(y, 8, stride=STRIP), :] = jnp.where(join_direct, a, b)
-        return 0
-
-    lax.fori_loop(0, STRIP, put, 0, unroll=8)
-
-    def stores():
-        return [
-            pltpu.make_async_copy(
-                wout.at[pl.ds((h * 4 + f) * STRIP, STRIP)],
-                wave_ref.at[0, f, :, pl.ds(h * 128, 128)],
-                out_sem.at[h * 4 + f],
-            )
-            for h in range(2)
-            for f in range(4)
-        ]
-
-    for c in stores():
-        c.start()
     correlate(TURNS - 1)
-    half_idx = lax.shift_right_logical(lane, 1)
-    even_lane = jnp.bitwise_and(lane, 1) == 0
-    for o in range(OFFSETS):
-        for b in range(STRIP // 8):
-            e, q = img[0, o, b], img[1, o, b]
-            for h in range(2):
-                images_ref[0, o, pl.ds(8 * b, 8), pl.ds(128 * h, 128)] = jnp.where(
-                    even_lane, lane_gather(e, half_idx + 64 * h), lane_gather(q, half_idx + 64 * h)
-                )
 
     @pl.when(has_up)
     def _():
@@ -437,8 +412,6 @@
 
     for t in range(TURNS - 1):
         for_each_send(t, lambda c: c.wait_send())
-    for c in stores():
-        c.wait()
 
 
 def local(in_flight, entering, classes, freq_phase, class_slowness):
@@ -469,10 +442,7 @@
             pltpu.VMEM((KEPT, 2, 8, 128), i32),
             pltpu.VMEM((TURNS, TERMS, 8, 128), f32),
             pltpu.VMEM((8 * PLANE, 128), f32),
-            pltpu.VMEM((2, OFFSETS, STRIP // 8, 8, 128), f32),
-            pltpu.VMEM((8 * STRIP, 128), f32),
             dma((TURNS + 1, 8)),
-            dma((8,)),
             dma((TURNS - 1, 3)),
             dma((TURNS, 3)),
             dma((TURNS, 2)),

time: 38.5 us -> 38.1 us (0.990)
  Pallas kernels: 36.3 us -> 35.9 us
    pallas_call x1, Pallas kernels: 36.3 us -> 35.9 us  [local(): pl.pallas_call(kernel, out_shape=(pltpu.VMEM((1, OFFSETS, STRIP, 256), f3...]
where the time goes in v2:
time: 38.1 us; the launch traced here: 37.9 us
  Pallas kernels  35.9 us (94%)
  local copies, waits for them, and re-layouts  1.36 us (4%)
  between operations  0.64 us (2%)
    pallas_call x1, Pallas kernels, local(): pl.pallas_call(kernel, out_shape=(pltpu.VMEM((1, OFFSETS, STRIP, 256), f3...  35.9 us
    unnamed x2, local copies, waits for them, and re-layouts  1.36 us

profile of v2, /device:TPU:22, one launch (start us, length us, event | category | flops | bytes accessed | tf_op | source)
XLA Modules:
  0.0 37.9 jit_solution(8079023956730925860)
XLA Ops:
  0.6 35.9 %shard_map.68 = (f32[1,8,32,256]{3,2,1,0:T(8,128)S(1)}, f32[1,4,32,256]{3,2,1,0:T(8,128)S(1)}) custom-call(f32[1,4,32,256]{3,2,1,0:T(8,128)} %inflight_ref.1, f32[2,4,32,256]{3,2,1,0:T(8,128)} %entering_ref.1, s32[1,32,256]{2,1,0:T(8,128)} %classes_ref.1, f32[66]{0:T(128)} %freq_ref.1, f32[32]{0:T(128)} %slow_ref.1), custom_call_target="tpu_custom_call" | custom-call | flops 60000000 | bytes 1000000 | tf_op jit(solution)/shard_map/pallas_call | solution.py:422
  36.6 0.7 %copy.9 = f32[1,8,32,256]{3,2,1,0:T(8,128)} copy(f32[1,8,32,256]{3,2,1,0:T(8,128)S(1)} %get-tuple-element.2) | data formatting | bytes 524288
  37.3 0.7 %copy.10 = f32[1,4,32,256]{3,2,1,0:T(8,128)} copy(f32[1,4,32,256]{3,2,1,0:T(8,128)S(1)} %get-tuple-element.3) | data formatting | bytes 262144
